TPU v7x, 512 devices: a whole 4x4x16 slice. The times are simulated.
512 devices in a mesh: wide: 64 (over z, x_lo, core), narrow: 8 (over x_hi, y).
Axes of the slice: x: 4 (x_hi: 2, x_lo: 2; x = x_hi * 2 + x_lo), y: 4, z: 16, core: 2. Of those that a mesh axis runs over, the one named last changes fastest.
Arguments:
- b_blocks: bfloat16 [512, 1024, 1024], P(('wide', 'narrow')), may hold values from -6 to 6
- occ_energy: float32 [512], P(('wide', 'narrow')), may hold values from -1.2 to -0.4
- vir_energy: float32 [1024], replicated, may hold values from 0.2 to 3
- coef_vir: bfloat16 [1024, 1024], P('narrow'), may hold values from -3 to 3
Outputs:
- density: float32 [1024, 1024], P('wide', 'narrow')
- gamma_ao: bfloat16 [512, 1024, 1024], P('wide', 'narrow')
All inputs are finite; a program needn't handle non-finite values.
Results may differ from a plain program's by a relative error of at most 0.015.
Values may be sent and summed in bfloat16 or wider, within the bound.
A program may use at most 64 MiB of HBM per device.

v0:
```python
import jax
import jax.numpy as jnp
from jax import lax
from jax.sharding import PartitionSpec as P

NV = 1024
NAUX = 1024
SLAB = 256
STEPS = 3


def passed_along(shard, axis, by):
    peers = lax.axis_size(axis)
    return lax.ppermute(shard, axis, [(i, (i + by) % peers) for i in range(peers)])


def pair_step(b_own, e_own, vir_energy, slab, e_part, start, gamma, dens):
    coupling = lax.dot_general(
        b_own, slab, (((1,), (1,)), ((), ())), preferred_element_type=jnp.float32
    )
    e_slab = vir_energy[start : start + SLAB]
    denom = e_own + e_part - vir_energy[:, None] - e_slab[None, :]
    amplitude = (coupling / denom).astype(jnp.bfloat16)
    gamma = gamma + jnp.dot(amplitude, slab, preferred_element_type=jnp.float32)
    dens = dens + lax.dot_general(
        amplitude, amplitude, (((1,), (1,)), ((), ())), preferred_element_type=jnp.float32
    )
    return (gamma, dens)


def on_device(b_blocks, occ_energy, vir_energy, coef_vir):
    b_own = b_blocks[0]
    wide_count = lax.axis_size("wide")
    narrow_count = lax.axis_size("narrow")
    slab_count = NV // SLAB
    starts = [(step - 1) % slab_count * SLAB for step in range(1, STEPS + 1)]
    gamma = jnp.zeros((NV, NAUX), jnp.float32)
    dens = jnp.zeros((NV, NV), jnp.float32)
    for step in range(1, STEPS + 1):
        start = starts[step - 1]
        slab, energy = (
            passed_along(b_own[start : start + SLAB], "wide", step),
            passed_along(occ_energy.astype(jnp.bfloat16), "wide", step).astype(occ_energy.dtype),
        )
        gamma, dens = pair_step(b_own, occ_energy, vir_energy, slab, energy, start, gamma, dens)
    scale = 1.0 / (wide_count * narrow_count * STEPS)
    rows = lax.psum_scatter(dens, "wide", scatter_dimension=0, tiled=True)
    tile = lax.psum_scatter(
        rows.astype(jnp.bfloat16), "narrow", scatter_dimension=1, tiled=True
    ).astype(jnp.float32)
    density = tile * scale
    aux_cols = NAUX // narrow_count
    shaped = gamma.astype(jnp.bfloat16).reshape(NV, 1, narrow_count, aux_cols)
    moved = lax.all_to_all(shaped, "narrow", split_axis=2, concat_axis=1, tiled=True)
    gamma_ao = jnp.einsum(
        "akzq,na->kqn",
        moved,
        lax.all_gather(coef_vir, "narrow", axis=0, tiled=True),
        preferred_element_type=jnp.float32,
    ).astype(jnp.bfloat16)
    return (density, gamma_ao)


def solution(mesh):
    return jax.shard_map(
        on_device,
        mesh=mesh,
        in_specs=(P(("wide", "narrow"), None, None), P(("wide", "narrow")), P(), P("narrow", None)),
        out_specs=(P("wide", "narrow"), P("wide", "narrow", None)),
        check_vma=False,
    )
```

profile of v0, /device:TPU:6, one launch (start us, length us, event | category | flops | bytes accessed | tf_op | source)
XLA Modules:
  0.0 394.0 jit_solution(9614827607907360516)
XLA Ops:
  8.0 0.0 copy-start
  8.0 0.0 copy-start.8
  8.0 0.0 reduce-scatter.5.cloned.1.call-start
  8.1 1.6 slice_bitcast_fusion
  9.7 4.1 %collective-permute-start.2 = (bf16[256,1024]{1,0:T(8,128)(2,1)S(1)}, bf16[256,1024]{1,0:T(8,128)(2,1)S(1)}, u32[]{:S(2)}, u32[]{:S(2)}) collective-permute-start(bf16[256,1024]{1,0:T(8,128)(2,1)S(1)} %get-tuple-element.4), channel_id=1, source_target_pairs={{0,16},{8,24},{16,32},{24,40},{32,48},{40,56},{48,64},{56,72},{64,... | collective-permute-start | bytes 1572872 | tf_op jit(solution)/shard_map/ppermute | solution.py:14
  14.5 2.7 collective-permute-start.1
  17.2 7.8 %collective-permute-start.3 = (bf16[1]{0:T(256)(128)(2,1)}, bf16[1]{0:T(256)(128)(2,1)}, u32[]{:S(2)}, u32[]{:S(2)}) collective-permute-start(bf16[1]{0:T(256)(128)(2,1)} %convert_element_type.36), channel_id=1, source_target_pairs={{0,16},{8,24},{16,32},{24,40},{32,48},{40,56},{48,64},{56,72},{64,... | collective-permute-start | bytes 14 | tf_op jit(solution)/shard_map/ppermute | solution.py:14
  25.0 7.5 %collective-permute-start.5 = (bf16[1]{0:T(256)(128)(2,1)}, bf16[1]{0:T(256)(128)(2,1)}, u32[]{:S(2)}, u32[]{:S(2)}) collective-permute-start(bf16[1]{0:T(256)(128)(2,1)} %convert_element_type.36), channel_id=1, source_target_pairs={{0,24},{8,32},{16,40},{24,48},{32,56},{40,64},{48,72},{56,80},{64,... | collective-permute-start | bytes 14 | tf_op jit(solution)/shard_map/ppermute | solution.py:14
  32.5 1.9 collective-permute-start
  34.4 0.0 copy-done.8
  34.4 0.0 collective-permute-done.1
  34.4 5.0 %collective-permute-start.4 = (bf16[256,1024]{1,0:T(8,128)(2,1)S(1)}, bf16[256,1024]{1,0:T(8,128)(2,1)S(1)}, u32[]{:S(2)}, u32[]{:S(2)}) collective-permute-start(bf16[256,1024]{1,0:T(8,128)(2,1)S(1)} %get-tuple-element.2), channel_id=1, source_target_pairs={{0,24},{8,32},{16,40},{24,48},{32,56},{40,64},{48,72},{56,80},{64,... | collective-permute-start | bytes 1572872 | tf_op jit(solution)/shard_map/ppermute | solution.py:14
  40.1 0.0 collective-permute-done.3
  40.7 0.0 collective-permute-done.5
  41.4 0.0 collective-permute-done.2
  41.4 0.0 copy-start.2
  41.4 0.0 copy-done
  41.4 0.7 fusion.23
  42.2 0.0 copy-done.2
  42.2 2.9 collective-permute-done
  45.1 0.0 copy-start.4
  45.1 0.8 copy-done.4
  45.9 0.7 fusion.17
  46.6 0.7 fusion.34
  47.4 0.0 copy-start.1
  47.4 0.7 fusion.33
  48.1 8.6 %collective-permute-done.4 = bf16[256,1024]{1,0:T(8,128)(2,1)S(1)} collective-permute-done((bf16[256,1024]{1,0:T(8,128)(2,1)S(1)}, bf16[256,1024]{1,0:T(8,128)(2,1)S(1)}, u32[]{:S(2)}, u32[]{:S(2)}) %collective-permute-start.4) | collective-permute-done | bytes 524320 | tf_op jit(solution)/shard_map/ppermute | solution.py:14
  56.7 0.0 copy-start.6
  56.7 0.8 copy-done.6
  57.5 0.0 copy-done.1
  57.5 0.7 fusion.29
  58.3 2.7 add_add_fusion
  61.0 0.0 copy-start.3
  61.0 0.0 reduce-scatter.5.cloned.1.call-update
  61.0 0.0 all-gather.2.cloned.1.call-start
  61.0 0.5 all-gather.2.cloned.1.call-update
  61.6 0.4 copy-done.3
  62.0 0.0 copy-start.5
  62.0 0.8 fusion.36
  62.8 0.3 copy-done.5
  63.1 0.0 copy-start.7
  63.1 0.8 fusion.35
  63.8 0.3 copy-done.7
  64.1 2.1 add_convert_fusion
  66.2 7.4 %all-to-all-start = ((bf16[1024,1,8,128]{0,3,1,2:T(8,128)(2,1)}), bf16[1024,1,8,128]{0,3,1,2:T(8,128)(2,1)S(1)}, u32[]{:S(2)}, u32[]{:S(2)}) async-start(bf16[1024,1,8,128]{0,3,1,2:T(8,128)(2,1)} %bitcast.8), calls=%async_computation.1 | async-start | bytes 4194304 | tf_op jit(solution)/shard_map/all_to_all | solution.py:54
  73.6 0.0 reduce-scatter.7.cloned.1.call-start
  73.6 223.8 %reduce-scatter.5.cloned.1.call-done = f32[16,1024]{1,0:T(8,128)} async-done(((f32[1024,1024]{1,0:T(8,128)}), f32[16,1024]{1,0:T(8,128)}) %reduce-scatter.5.cloned.1.call-update) | async-done | bytes 65552 | tf_op jit(solution)/shard_map/reduce_scatter | solution.py:47
  297.4 0.8 convert_element_type.43
  298.2 0.8 copy.7
  299.1 0.0 reduce-scatter.7.cloned.1.call-update
  299.1 0.0 all-to-all-done
  299.1 0.0 all-gather.2.cloned.1.call-done
  299.2 5.3 %fusion.9 = bf16[8,128,1024]{2,1,0:T(8,128)(2,1)} fusion(bf16[1024,1024]{1,0:T(8,128)(2,1)} %all-gather.2.cloned.1.call-done, bf16[1024,1,8,128]{0,3,1,2:T(8,128)(2,1)S(1)} %all-to-all-done), kind=kOutput, calls=%fused_computation.11 | convolution fusion | flops 2148532224 | bytes 6291456 | tf_op jit(solution)/shard_map/akzq,na->kqn/dot_general | solution.py:55
  304.4 80.6 %reduce-scatter.7.cloned.1.call-done = bf16[128,16]{1,0:T(8,128)(2,1)} async-done(((bf16[1024,16]{1,0:T(8,128)(2,1)}), bf16[128,16]{1,0:T(8,128)(2,1)}) %reduce-scatter.7.cloned.1.call-update) | async-done | bytes 4112
  385.1 0.8 copy.8
  385.9 0.6 convert_multiply_fusion
  (2 shorter events, 0.0 us)
Async XLA Ops:
  8.0 33.4 %copy-start = (bf16[1,1024,1024]{2,1,0:T(8,128)(2,1)S(1)}, bf16[1,1024,1024]{2,1,0:T(8,128)(2,1)}, u32[]{:S(2)}) copy-start(bf16[1,1024,1024]{2,1,0:T(8,128)(2,1)} %param.4) | copy-start | bytes 6291460
  8.0 26.4 %copy-start.8 = (f32[1024]{0:T(1024)S(1)}, f32[1024]{0:T(1024)}, u32[]{:S(2)}) copy-start(f32[1024]{0:T(1024)} %param.6) | copy-start | bytes 12292
  8.0 289.4 %reduce-scatter.5.cloned.1.call-start = ((), (), s32[]{:S(2)}) async-start(), calls=%async_computation.3 | async-start | bytes 4259840 | tf_op jit(solution)/shard_map/reduce_scatter | solution.py:47
  9.7 31.7 %collective-permute-start.2 = (bf16[256,1024]{1,0:T(8,128)(2,1)S(1)}, bf16[256,1024]{1,0:T(8,128)(2,1)S(1)}, u32[]{:S(2)}, u32[]{:S(2)}) collective-permute-start(bf16[256,1024]{1,0:T(8,128)(2,1)S(1)} %get-tuple-element.4), channel_id=1, source_target_pairs={{0,16},{8,24},{16,32},{24,40},{32,48},{40,56},{48,64},{56,72},{64,... | collective-permute-start | bytes 1572872 | tf_op jit(solution)/shard_map/ppermute | solution.py:14
  14.5 19.9 %collective-permute-start.1 = (bf16[1]{0:T(256)(128)(2,1)}, bf16[1]{0:T(256)(128)(2,1)}, u32[]{:S(2)}, u32[]{:S(2)}) collective-permute-start(bf16[1]{0:T(256)(128)(2,1)} %convert_element_type.36), channel_id=1, source_target_pairs={{0,8},{8,16},{16,24},{24,32},{32,40},{40,48},{48,56},{56,64},{64,7... | collective-permute-start | bytes 14 | tf_op jit(solution)/shard_map/ppermute | solution.py:14
  17.2 22.9 %collective-permute-start.3 = (bf16[1]{0:T(256)(128)(2,1)}, bf16[1]{0:T(256)(128)(2,1)}, u32[]{:S(2)}, u32[]{:S(2)}) collective-permute-start(bf16[1]{0:T(256)(128)(2,1)} %convert_element_type.36), channel_id=1, source_target_pairs={{0,16},{8,24},{16,32},{24,40},{32,48},{40,56},{48,64},{56,72},{64,... | collective-permute-start | bytes 14 | tf_op jit(solution)/shard_map/ppermute | solution.py:14
  25.0 15.7 %collective-permute-start.5 = (bf16[1]{0:T(256)(128)(2,1)}, bf16[1]{0:T(256)(128)(2,1)}, u32[]{:S(2)}, u32[]{:S(2)}) collective-permute-start(bf16[1]{0:T(256)(128)(2,1)} %convert_element_type.36), channel_id=1, source_target_pairs={{0,24},{8,32},{16,40},{24,48},{32,56},{40,64},{48,72},{56,80},{64,... | collective-permute-start | bytes 14 | tf_op jit(solution)/shard_map/ppermute | solution.py:14
  32.5 12.6 %collective-permute-start = (bf16[256,1024]{1,0:T(8,128)(2,1)S(1)}, bf16[256,1024]{1,0:T(8,128)(2,1)S(1)}, u32[]{:S(2)}, u32[]{:S(2)}) collective-permute-start(bf16[256,1024]{1,0:T(8,128)(2,1)S(1)} %get-tuple-element.3), channel_id=1, source_target_pairs={{0,8},{8,16},{16,24},{24,32},{32,40},{40,48},{48,56},{56,64},{64,7... | collective-permute-start | bytes 1572872 | tf_op jit(solution)/shard_map/ppermute | solution.py:14
  34.4 22.3 %collective-permute-start.4 = (bf16[256,1024]{1,0:T(8,128)(2,1)S(1)}, bf16[256,1024]{1,0:T(8,128)(2,1)S(1)}, u32[]{:S(2)}, u32[]{:S(2)}) collective-permute-start(bf16[256,1024]{1,0:T(8,128)(2,1)S(1)} %get-tuple-element.2), channel_id=1, source_target_pairs={{0,24},{8,32},{16,40},{24,48},{32,56},{40,64},{48,72},{56,80},{64,... | collective-permute-start | bytes 1572872 | tf_op jit(solution)/shard_map/ppermute | solution.py:14
  41.4 0.8 copy-start.2
  45.1 0.8 copy-start.4
  47.4 10.2 %copy-start.1 = (bf16[1,1024,1024]{2,1,0:T(8,128)(2,1)S(1)}, bf16[1,1024,1024]{2,1,0:T(8,128)(2,1)}, u32[]{:S(2)}) copy-start(bf16[1,1024,1024]{2,1,0:T(8,128)(2,1)} %param.4) | copy-start | bytes 6291460
  56.7 0.8 copy-start.6
  61.0 1.0 copy-start.3
  61.0 238.2 %all-gather.2.cloned.1.call-start = ((), (), s32[]{:S(2)}) async-start(), calls=%async_computation.4 | async-start | bytes 2359296 | tf_op jit(solution)/shard_map/all_gather | solution.py:58
  62.0 1.0 copy-start.5
  63.1 1.0 copy-start.7
  66.2 232.9 %all-to-all-start = ((bf16[1024,1,8,128]{0,3,1,2:T(8,128)(2,1)}), bf16[1024,1,8,128]{0,3,1,2:T(8,128)(2,1)S(1)}, u32[]{:S(2)}, u32[]{:S(2)}) async-start(bf16[1024,1,8,128]{0,3,1,2:T(8,128)(2,1)} %bitcast.8), calls=%async_computation.1 | async-start | bytes 4194304 | tf_op jit(solution)/shard_map/all_to_all | solution.py:54
  73.6 311.5 %reduce-scatter.7.cloned.1.call-start = ((), (), s32[]{:S(2)}) async-start(), calls=%async_computation.5 | async-start | bytes 294912
Sparse Core Ops, SparseCore 0:
  61.1 236.2 reduce-scatter.4
Sparse Core Ops, SparseCore 1:
  64.7 75.1 all-gather.1
  299.2 85.8 reduce-scatter.6
where the time goes:
time: 395 us; the launch traced here: 394 us
  waiting for transfers between devices  317 us (80%)
  starting transfers between devices  36.5 us (9%)
  between operations  18.3 us (5%)
  matrix products  15.3 us (4%)
  local copies, waits for them, and re-layouts  5.92 us (1%)
    reduce_scatter x1, waiting for transfers between devices, on_device(): rows = lax.psum_scatter(dens, 'wide', scatter_dimension=0, tiled=True)  224 us
    unnamed x4, waiting for transfers between devices  81.2 us
    ppermute x6, starting transfers between devices, passed_along(): lax.ppermute(shard, axis, [(i, (i + by) % peers) for i in range(peers)])  29 us
    ppermute x6, waiting for transfers between devices, passed_along(): lax.ppermute(shard, axis, [(i, (i + by) % peers) for i in range(peers)])  11.5 us
  transfers between devices with their start and end apart: 10, of which 4 were waited for; matrix products, arithmetic and copies ran while one was open for 3% of the time, Pallas kernels for 0%

commit v1 on v0

v1 whole, which is shorter than its diff:
```python
import jax
import jax.numpy as jnp
from jax import lax
from jax.experimental import pallas as pl
from jax.experimental.pallas import tpu as pltpu
from jax.sharding import PartitionSpec as P

NV = 1024
NAUX = 1024
NAO = 1024
SLAB = 256
STEPS = 3
PAIRS = 512 * STEPS
MESH = pl.DeviceIdType.MESH
BF = jnp.bfloat16
F32 = jnp.float32
NT = (((1,), (1,)), ((), ()))
Y_ORDER = (2, 1, 3, 0)


def kernel(
    b_hbm,
    occ_ref,
    vir_ref,
    coef_hbm,
    dens_ref,
    gao_ref,
    b_vm,
    slab,
    e_own,
    e_part,
    cf,
    vcol,
    amp,
    tr,
    st,
    d_own,
    d_send,
    d_recv,
    dy_send,
    dy_recv,
    dsum,
    dx_send,
    dx_recv,
    dz,
    dl_send,
    dl_recv,
    dg,
    dg_recv,
    o_send,
    local_sem,
    e_ss,
    e_rs,
    s_ss,
    s_rs,
    c_ss,
    c_rs,
    f_ss,
    f_rs,
    dc_ss,
    dc_rs,
    dy_ss,
    dy_rs,
    dx_ss,
    dx_rs,
    dl_ss,
    dl_rs,
    dg_ss,
    dg_rs,
    o_ss,
    o_rs,
):
    w = lax.axis_index("wide")
    n = lax.axis_index("narrow")
    z, xlo, core = w // 4, (w // 2) % 2, w % 2
    xhi, y = n // 4, n % 4
    g, l = z // 4, z % 4

    def at(z_, xlo_, core_, xhi_, y_):
        return (z_ * 4 + xlo_ * 2 + core_, xhi_ * 4 + y_)

    started = []

    def send(src, dst, ss, rs, dev):
        copy = pltpu.make_async_remote_copy(
            src_ref=src, dst_ref=dst, send_sem=ss, recv_sem=rs, device_id=dev, device_id_type=MESH
        )
        copy.start()
        started.append(copy)
        return copy

    other = at(z, xlo, 1 - core, xhi, y)
    across = at(z, 1 - xlo, core, 1 - xhi, y)
    ydev = [None] + [at(z, xlo, core, xhi, (y + d) % 4) for d in (1, 2, 3)]
    xdev = [
        at(z, xlo, core, 1 - xhi, y),
        at(z, 1 - xlo, core, xhi, y),
        across,
    ]
    ldev = [None] + [at(g * 4 + (l + d) % 4, xlo, core, xhi, y) for d in (1, 2, 3)]
    gdev = [None] + [at((g + d) % 4 * 4 + l, xlo, core, xhi, y) for d in (1, 2, 3)]

    barrier = pltpu.get_barrier_semaphore()
    greet = [((w + 64 - s) % 64, n) for s in (1, 2, 3)]
    greet += [other] + xdev + ydev[1:] + ldev[1:] + gdev[1:]
    greet += [at(z, xlo, core, 1 - xhi, (y + d) % 4) for d in (1, 2, 3)]
    for dev in greet:
        pl.semaphore_signal(barrier, inc=1, device_id=dev, device_id_type=MESH)

    load_b = pltpu.make_async_copy(b_hbm.at[0], b_vm, local_sem.at[0])
    load_b.start()
    load_c = pltpu.make_async_copy(coef_hbm, cf.at[n], local_sem.at[1])
    load_c.start()
    e_own[...] = jnp.full((8, 128), occ_ref[0], F32)

    pl.semaphore_wait(barrier, len(greet))

    e_cp, s_cp = [], []
    for s in range(STEPS):
        dev = ((w + s + 1) % 64, n)
        e_cp.append(send(e_own, e_part.at[s], e_ss.at[s], e_rs.at[s], dev))
    for s in range(STEPS):
        dev = ((w + s + 1) % 64, n)
        start = s % (NV // SLAB) * SLAB
        s_cp.append(send(b_hbm.at[0, pl.ds(start, SLAB)], slab.at[s], s_ss.at[s], s_rs.at[s], dev))

    half = pl.ds(pl.multiple_of(core * 64, 64), 64)
    mine = coef_hbm.at[half]
    c_cp = [send(mine, cf.at[n, half], c_ss.at[0], c_rs.at[0], across)]
    for d in (1, 2, 3):
        c_cp.append(send(mine, cf.at[n, half], c_ss.at[d], c_rs.at[d], ydev[d]))

    for k in range(8):
        row = vir_ref[:, k * 128 : (k + 1) * 128]
        vcol[k * 128 : (k + 1) * 128, :] = jnp.broadcast_to(row, (128, 128)).T

    c_cp[0].wait_recv()
    far = cf.at[(1 - xhi) * 4 + y, half]
    for d in (1, 2, 3):
        c_cp.append(send(far, far, c_ss.at[3 + d], c_rs.at[3 + d], ydev[d]))
    f_cp = [send(far, far, f_ss.at[0], f_rs.at[0], other)]
    for d in (1, 2, 3):
        c_cp[d].wait_recv()
        piece = cf.at[xhi * 4 + (y + 4 - d) % 4, half]
        f_cp.append(send(piece, piece, f_ss.at[d], f_rs.at[d], other))

    load_b.wait()

    def couple(s):
        e_cp[s].wait_recv()
        s_cp[s].wait_recv()
        start = s % (NV // SLAB) * SLAB
        e_sum = (e_own[...] + e_part[s])[0:1, 0:1]
        e_slab = vir_ref[:, start : start + SLAB]

        def rows(r, _):
            a = pl.ds(pl.multiple_of(r * 256, 256), 256)
            c = lax.dot_general(b_vm[a, :], slab[s], NT, preferred_element_type=F32)
            denom = (e_sum - vcol[a, 0:1]) - e_slab
            amp[a, s * SLAB : (s + 1) * SLAB] = (c / denom).astype(BF)
            return 0

        lax.fori_loop(0, 4, rows, 0)

    def transform(s):
        cols = slice(s * SLAB, (s + 1) * SLAB)
        for k in range(4):
            st[k * 256 : (k + 1) * 256, cols] = slab[s, :, k * 256 : (k + 1) * 256].T

        def rows(r, _):
            cc = cf[pl.ds(r * 2, 2)].reshape(256, NV)
            t = jnp.dot(cc, amp[:, cols], preferred_element_type=F32)
            tr[pl.ds(pl.multiple_of(r * 256, 256), 256), cols] = t.astype(BF)
            return 0

        lax.fori_loop(0, 4, rows, 0)

    couple(0)

    for d in (1, 2, 3):
        c_cp[3 + d].wait_recv()
        piece = cf.at[(1 - xhi) * 4 + (y + 4 - d) % 4, half]
        f_cp.append(send(piece, piece, f_ss.at[3 + d], f_rs.at[3 + d], other))
    load_c.wait()
    for copy in f_cp:
        copy.wait_recv()

    transform(0)
    couple(1)
    transform(1)
    couple(2)

    dc_cp = []
    for q, d in enumerate(Y_ORDER):
        y_ = (y + d) % 4
        lo = pl.ds(pl.multiple_of(y_ * 128, 128), 128)
        hi = pl.ds(pl.multiple_of(512 + y_ * 128, 128), 128)

        def rows(r, _):
            right = jnp.concatenate([amp[lo, :], amp[hi, :]], axis=0)
            a = pl.ds(pl.multiple_of(r * 256, 256), 256)
            v = lax.dot_general(amp[a, :], right, NT, preferred_element_type=F32)
            v = v.reshape(8, 2, 16, 256)
            v0, v1 = v[:, 0], v[:, 1]
            first = core == 0
            d_own[q, pl.ds(r * 8, 8)] = jnp.where(first, v0, v1)
            d_send[q, pl.ds(r * 8, 8)] = jnp.where(first, v1, v0).astype(BF)
            return 0

        lax.fori_loop(0, 4, rows, 0)
        dc_cp.append(send(d_send.at[q], d_recv.at[q], dc_ss.at[q], dc_rs.at[q], other))

    transform(2)

    dy_cp = []
    for q, d in enumerate(Y_ORDER):
        dc_cp[q].wait_recv()
        if d:

            def add(r, _):
                k = pl.ds(r * 8, 8)
                dy_send[q, k] = (d_own[q, k] + d_recv[q, k].astype(F32)).astype(BF)
                return 0

            lax.fori_loop(0, 4, add, 0)
            dy_cp.append(send(dy_send.at[q], dy_recv.at[q], dy_ss.at[q], dy_rs.at[q], ydev[d]))

    o_cp = []
    own_copy = None
    for q, d in enumerate(Y_ORDER):
        y_ = (y + d) % 4
        lo = pl.ds(pl.multiple_of(y_ * 128, 128), 128)
        hi = pl.ds(pl.multiple_of(512 + y_ * 128, 128), 128)

        def cols(k, _):
            left = jnp.concatenate([st[lo, :], st[hi, :]], axis=0)
            m = pl.ds(pl.multiple_of(k * 256, 256), 256)
            v = lax.dot_general(left, tr[m, :], NT, preferred_element_type=F32)
            v = v.astype(BF)
            o_send[q, 0, :, m] = v[:128]
            o_send[q, 1, :, m] = v[128:]
            return 0

        lax.fori_loop(0, 4, cols, 0)
        i = 2 * q
        o_cp.append(
            send(o_send.at[q, 1 - xhi], gao_ref.at[n], o_ss.at[i], o_rs.at[i], at(z, xlo, core, 1 - xhi, y_))
        )
        if d:
            o_cp.append(
                send(o_send.at[q, xhi], gao_ref.at[n], o_ss.at[i + 1], o_rs.at[i + 1], at(z, xlo, core, xhi, y_))
            )
        else:
            own_copy = pltpu.make_async_copy(o_send.at[q, xhi], gao_ref.at[n], local_sem.at[2])
            own_copy.start()

    for copy in dy_cp:
        copy.wait_recv()

    def sum_y(r, _):
        k = pl.ds(r * 8, 8)
        v = d_own[3, k] + d_recv[3, k].astype(F32)
        for q in range(3):
            v = v + dy_recv[q, k].astype(F32)
        v = v.reshape(4, 2, 16, 256)
        k4 = pl.ds(r * 4, 4)
        for lo_ in range(2):
            for hi_ in range(2):
                dsum[hi_, lo_, k4] = v[:, lo_, :, hi_ * 128 : (hi_ + 1) * 128]
        return 0

    lax.fori_loop(0, 4, sum_y, 0)
    dx_cp = []
    for k, (hi_, lo_) in enumerate(((1 - xhi, xlo), (xhi, 1 - xlo), (1 - xhi, 1 - xlo))):
        dx_send[k] = dsum[hi_, lo_].astype(BF)
        dx_cp.append(send(dx_send.at[k], dx_recv.at[k], dx_ss.at[k], dx_rs.at[k], xdev[k]))
    for copy in dx_cp:
        copy.wait_recv()
    v = dsum[xhi, xlo]
    for k in range(3):
        v = v + dx_recv[k].astype(F32)
    dz[...] = v.reshape(4, 4, 16, 128)
    dl_cp = []
    for d in (1, 2, 3):
        dl_send[d - 1] = dz[:, (l + d) % 4].astype(BF)
        dl_cp.append(send(dl_send.at[d - 1], dl_recv.at[d - 1], dl_ss.at[d - 1], dl_rs.at[d - 1], ldev[d]))
    for copy in dl_cp:
        copy.wait_recv()
    v = dz[:, l]
    for k in range(3):
        v = v + dl_recv[k].astype(F32)
    dg[...] = v
    dg_cp = []
    for d in (1, 2, 3):
        dg_cp.append(send(dg.at[(g + d) % 4], dg_recv.at[d - 1], dg_ss.at[d - 1], dg_rs.at[d - 1], gdev[d]))
    for copy in dg_cp:
        copy.wait_recv()
    v = dg[g]
    for k in range(3):
        v = v + dg_recv[k]
    dens_ref[...] = v * (1.0 / PAIRS)

    own_copy.wait()
    for copy in o_cp:
        copy.wait_recv()
    for copy in started:
        copy.wait_send()


def on_device(b_blocks, occ_energy, vir_energy, coef_vir):
    dma = pltpu.SemaphoreType.DMA
    vm = pltpu.VMEM
    scratch = [
        vm((NV, NAUX), BF),
        vm((STEPS, SLAB, NAUX), BF),
        vm((8, 128), F32),
        vm((STEPS, 8, 128), F32),
        vm((8, 128, NV), BF),
        vm((NV, 128), F32),
        vm((NV, STEPS * SLAB), BF),
        vm((NAO, STEPS * SLAB), BF),
        vm((NAUX, STEPS * SLAB), BF),
        vm((4, 32, 16, 256), F32),
        vm((4, 32, 16, 256), BF),
        vm((4, 32, 16, 256), BF),
        vm((3, 32, 16, 256), BF),
        vm((3, 32, 16, 256), BF),
        vm((2, 2, 16, 16, 128), F32),
        vm((3, 16, 16, 128), BF),
        vm((3, 16, 16, 128), BF),
        vm((4, 4, 16, 128), F32),
        vm((3, 4, 16, 128), BF),
        vm((3, 4, 16, 128), BF),
        vm((4, 16, 128), F32),
        vm((3, 16, 128), F32),
        vm((4, 2, 128, NAO), BF),
        dma((3,)),
    ]
    for count in (3, 3, 7, 7, 4, 3, 3, 3, 3, 8):
        scratch += [dma((count,)), dma((count,))]
    return pl.pallas_call(
        kernel,
        out_shape=(
            jax.ShapeDtypeStruct((16, 128), F32),
            jax.ShapeDtypeStruct((8, 128, NAO), BF),
        ),
        in_specs=[
            pl.BlockSpec(memory_space=pl.ANY),
            pl.BlockSpec(memory_space=pltpu.SMEM),
            pl.BlockSpec(memory_space=pltpu.VMEM),
            pl.BlockSpec(memory_space=pl.ANY),
        ],
        out_specs=(
            pl.BlockSpec(memory_space=pltpu.VMEM),
            pl.BlockSpec(memory_space=pl.ANY),
        ),
        scratch_shapes=scratch,
        compiler_params=pltpu.CompilerParams(
            collective_id=0, has_side_effects=True, vmem_limit_bytes=48 * 1024 * 1024
        ),
    )(b_blocks, occ_energy, vir_energy.reshape(1, NV), coef_vir)


def solution(mesh):
    return jax.shard_map(
        on_device,
        mesh=mesh,
        in_specs=(P(("wide", "narrow"), None, None), P(("wide", "narrow")), P(), P("narrow", None)),
        out_specs=(P("wide", "narrow"), P("wide", "narrow", None)),
        check_vma=False,
    )
```

time: 395 us -> 101 us (0.26)
  the two profiles are of different devices: /device:TPU:6 before, /device:TPU:32 now
where the time goes in v1:
time: 101 us
  Pallas kernels  94.3 us (93%)
  local copies, waits for them, and re-layouts  5.14 us (5%)
  between operations  1.29 us (1%)
    pallas_call x1, Pallas kernels, on_device(): pl.pallas_call(kernel, out_shape=(jax.ShapeDtypeStruct((16, 128), F32), j...  94.3 us
    unnamed x8, local copies, waits for them, and re-layouts  5.14 us

profile of v1, /device:TPU:32, one launch (start us, length us, event | category | flops | bytes accessed | tf_op | source)
XLA Modules:
  0.0 100.7 jit_solution(685904238164684320)
XLA Ops:
  1.3 0.0 copy-start
  1.3 1.6 %copy-done = bf16[1,1024,1024]{2,1,0:T(8,128)(2,1)S(1)} copy-done((bf16[1,1024,1024]{2,1,0:T(8,128)(2,1)S(1)}, bf16[1,1024,1024]{2,1,0:T(8,128)(2,1)}, u32[]{:S(2)}) %copy-start) | copy-done | bytes 2097176
  2.9 0.0 copy-start.1
  2.9 0.9 copy-done.1
  3.8 0.0 copy-start.2
  3.8 0.7 copy-done.2
  4.5 94.3 %shard_map.59 = (f32[16,128]{1,0:T(8,128)S(1)}, bf16[8,128,1024]{2,1,0:T(8,128)(2,1)S(1)}) custom-call(bf16[1,1024,1024]{2,1,0:T(8,128)(2,1)S(1)} %copy-done, f32[1]{0:T(128)S(6)} %copy.8.occ_ref, f32[1,1024]{1,0:T(1,128)S(1)} %bitcast.1, bf16[128,1024]{1,0:T(8,128)(2,1)S(1)} %copy-done.1), custom_call_target="tpu_custom_call" | custom-call | tf_op jit(solution)/shard_map/pallas_call | solution.py:341
  98.8 0.6 copy.9
  99.4 1.3 %copy.10 = bf16[8,128,1024]{2,1,0:T(8,128)(2,1)} copy(bf16[8,128,1024]{2,1,0:T(8,128)(2,1)S(1)} %get-tuple-element.5) | data formatting | bytes 4194304
Async XLA Ops:
  1.3 1.6 %copy-start = (bf16[1,1024,1024]{2,1,0:T(8,128)(2,1)S(1)}, bf16[1,1024,1024]{2,1,0:T(8,128)(2,1)}, u32[]{:S(2)}) copy-start(bf16[1,1024,1024]{2,1,0:T(8,128)(2,1)} %b_hbm.1) | copy-start | bytes 6291460
  2.9 0.9 copy-start.1
  3.8 0.7 copy-start.2

commit v2 on v1

v2 whole, which is shorter than its diff:
```python
import jax
import jax.numpy as jnp
from jax import lax
from jax.experimental import pallas as pl
from jax.experimental.pallas import tpu as pltpu
from jax.sharding import PartitionSpec as P

NV = 1024
NAUX = 1024
NAO = 1024
SLAB = 256
STEPS = 3
PAIRS = 512 * STEPS
MESH = pl.DeviceIdType.MESH
BF = jnp.bfloat16
F32 = jnp.float32
NT = (((1,), (1,)), ((), ()))
Y_ORDER = (2, 1, 3, 0)


def kernel(
    b_hbm,
    occ_ref,
    vir_hbm,
    coef_hbm,
    dens_ref,
    gao_ref,
    b_vm,
    slab,
    e_own,
    e_part,
    cf,
    vcol,
    amp,
    tr,
    st,
    d_own,
    d_send,
    d_recv,
    y1_send,
    y1_recv,
    x1_send,
    x1_recv,
    e0,
    e1,
    x2_send,
    x2_recv,
    y2_send,
    y2_recv,
    dz,
    dl_send,
    dl_recv,
    dg,
    dg_recv,
    vir_ref,
    o_send,
    d_acc,
    word,
    local_sem,
    e_ss,
    e_rs,
    s_ss,
    s_rs,
    c_ss,
    c_rs,
    f_ss,
    f_rs,
    dc_ss,
    dc_rs,
    y1_ss,
    y1_rs,
    x1_ss,
    x1_rs,
    x2_ss,
    x2_rs,
    y2_ss,
    y2_rs,
    dl_ss,
    dl_rs,
    dg_ss,
    dg_rs,
    o_ss,
    o_rs,
    r_ss,
    r_rs,
):
    w = lax.axis_index("wide")
    n = lax.axis_index("narrow")
    z, xlo, core = w // 4, (w // 2) % 2, w % 2
    xhi, y = n // 4, n % 4
    g, l = z // 4, z % 4

    def at(z_, xlo_, core_, xhi_, y_):
        return (z_ * 4 + xlo_ * 2 + core_, xhi_ * 4 + y_)

    started = []

    def send(src, dst, ss, rs, dev):
        copy = pltpu.make_async_remote_copy(
            src_ref=src, dst_ref=dst, send_sem=ss, recv_sem=rs, device_id=dev, device_id_type=MESH
        )
        copy.start()
        started.append(copy)
        return copy

    other = at(z, xlo, 1 - core, xhi, y)
    across = at(z, 1 - xlo, core, 1 - xhi, y)
    ydev = [None] + [at(z, xlo, core, xhi, (y + d) % 4) for d in (1, 2, 3)]
    xdev = [
        at(z, xlo, core, 1 - xhi, y),
        at(z, 1 - xlo, core, xhi, y),
        across,
    ]
    ldev = [None] + [at(g * 4 + (l + d) % 4, xlo, core, xhi, y) for d in (1, 2, 3)]
    gdev = [None] + [at((g + d) % 4 * 4 + l, xlo, core, xhi, y) for d in (1, 2, 3)]

    barrier = pltpu.get_barrier_semaphore()
    greet = [((w + 64 - s) % 64, n) for s in (1, 2, 3, 4)]
    greet += [((w + 2) % 64, n), ((w + 4) % 64, n)]
    greet += [other] + xdev + ydev[1:]
    for dev in greet:
        pl.semaphore_signal(barrier, inc=1, device_id=dev, device_id_type=MESH)

    load_b = pltpu.make_async_copy(b_hbm.at[0], b_vm, local_sem.at[0])
    load_b.start()
    load_c = pltpu.make_async_copy(coef_hbm, cf.at[n], local_sem.at[1])
    load_c.start()
    load_v = pltpu.make_async_copy(vir_hbm, vir_ref, local_sem.at[3])
    load_v.start()
    e_own[...] = jnp.full((8, 128), occ_ref[0], F32)

    pl.semaphore_wait(barrier, len(greet))

    def pass_word(k, devs):
        for dev in devs:
            pl.semaphore_signal(word.at[k], inc=1, device_id=dev, device_id_type=MESH)

    def along(d):
        return [((w + 4 * d) % 64, n), ((w + 64 - 4 * d) % 64, n)]

    e_cp = []
    for s in range(STEPS):
        dev = ((w + s + 1) % 64, n)
        e_cp.append(send(e_own, e_part.at[s], e_ss.at[s], e_rs.at[s], dev))
    s_early, s_late = core * 2, 2 - core * 2
    r_early, r_late = 2 - core * 2, core * 2

    def slab_copy(s):
        return pltpu.make_async_remote_copy(
            src_ref=b_hbm.at[0, pl.ds(pl.multiple_of(s * SLAB, SLAB), SLAB)],
            dst_ref=slab.at[s],
            send_sem=s_ss.at[s],
            recv_sem=s_rs.at[s],
            device_id=((w + s + 1) % 64, n),
            device_id_type=MESH,
        )

    def quarter(k):
        return pltpu.make_async_remote_copy(
            src_ref=b_hbm.at[0, pl.ds(SLAB + k * 64, 64)],
            dst_ref=slab.at[1, pl.ds(k * 64, 64)],
            send_sem=r_ss.at[k],
            recv_sem=r_rs.at[4 + k],
            device_id=((w + 2) % 64, n),
            device_id_type=MESH,
        )

    for k in range(4):
        quarter(k).start()

    slab_copy(s_early).start()
    slab_copy(s_late).start()
    pass_word(0, along(1))
    pass_word(3, [xdev[0]])

    half = pl.ds(pl.multiple_of(core * 64, 64), 64)
    mine = coef_hbm.at[half]
    c_cp = [send(mine, cf.at[n, half], c_ss.at[0], c_rs.at[0], across)]
    for d in (1, 2, 3):
        c_cp.append(send(mine, cf.at[n, half], c_ss.at[d], c_rs.at[d], ydev[d]))

    load_v.wait()
    for k in range(8):
        row = vir_ref[:, k * 128 : (k + 1) * 128]
        vcol[k * 128 : (k + 1) * 128, :] = jnp.broadcast_to(row, (128, 128)).T

    c_cp[0].wait_recv()
    far = cf.at[(1 - xhi) * 4 + y, half]
    for d in (1, 2, 3):
        c_cp.append(send(far, far, c_ss.at[3 + d], c_rs.at[3 + d], ydev[d]))
    f_cp = [send(far, far, f_ss.at[0], f_rs.at[0], other)]
    pl.semaphore_wait(word.at[0], 2)
    pass_word(1, along(2))
    for d in (1, 2, 3):
        c_cp[d].wait_recv()
        piece = cf.at[xhi * 4 + (y + 4 - d) % 4, half]
        f_cp.append(send(piece, piece, f_ss.at[d], f_rs.at[d], other))
    pl.semaphore_wait(word.at[1], 2)
    pass_word(2, along(4))
    load_b.wait()

    def couple(slot, s):
        if slot == 0:
            for copy in e_cp:
                copy.wait_recv()
        if slot == 1:
            for k in range(4):
                quarter(k).wait_recv()
        else:
            slab_copy(s).wait_recv()
        e_sum = (e_own[...] + e_part[s])[0:1, 0:1]
        e_slab = vir_ref[:, pl.ds(pl.multiple_of(s * SLAB, SLAB), SLAB)]
        c = lax.dot_general(b_vm[...], slab[s], NT, preferred_element_type=F32)
        denom = (e_sum - vcol[:, 0:1]) - e_slab
        amp[:, slot * SLAB : (slot + 1) * SLAB] = (c / denom).astype(BF)

    def transform(slot, s):
        cols = slice(slot * SLAB, (slot + 1) * SLAB)
        for k in range(4):
            st[k * 256 : (k + 1) * 256, cols] = slab[s, :, k * 256 : (k + 1) * 256].T

        t = jnp.dot(cf[...].reshape(NAO, NV), amp[:, cols], preferred_element_type=F32)
        tr[:, cols] = t.astype(BF)

    couple(0, r_early)

    for d in (1, 2, 3):
        c_cp[3 + d].wait_recv()
        piece = cf.at[(1 - xhi) * 4 + (y + 4 - d) % 4, half]
        f_cp.append(send(piece, piece, f_ss.at[3 + d], f_rs.at[3 + d], other))
    load_c.wait()
    for copy in f_cp:
        copy.wait_recv()

    transform(0, r_early)
    couple(1, 1)
    transform(1, 1)

    def columns(d):
        y_ = (y + d) % 4
        return (y_, pl.ds(pl.multiple_of(y_ * 128, 128), 128), pl.ds(pl.multiple_of(512 + y_ * 128, 128), 128))

    for q, d in enumerate(Y_ORDER):
        _, lo, hi = columns(d)
        right = jnp.concatenate([amp[lo, : 2 * SLAB], amp[hi, : 2 * SLAB]], axis=0)
        d_acc[q] = lax.dot_general(amp[:, : 2 * SLAB], right, NT, preferred_element_type=F32)
    couple(2, r_late)

    top, low = pl.ds(8, 8), pl.ds(0, 8)
    dt_cp, dc_cp = [], []
    for q, d in enumerate(Y_ORDER):
        y_, lo, hi = columns(d)
        right = jnp.concatenate([amp[lo, 2 * SLAB :], amp[hi, 2 * SLAB :]], axis=0)
        v = d_acc[q] + lax.dot_general(amp[:, 2 * SLAB :], right, NT, preferred_element_type=F32)
        v = v.reshape(16, 2, 2, 16, 256)
        v0, v1 = v[:, :, 0], v[:, :, 1]
        keep = jnp.where(core == 0, v0, v1)
        give = jnp.where(core == 0, v1, v0).astype(BF)
        for h in range(2):
            for x_ in range(2):
                d_own[y_, h, x_] = keep[:, x_, :, h * 128 : (h + 1) * 128]
                d_send[y_, h, x_] = give[:, x_, :, h * 128 : (h + 1) * 128]
        i = 2 * q
        dt_cp.append(send(d_send.at[y_, :, :, top], d_recv.at[y_, :, :, top], dc_ss.at[i], dc_rs.at[i], other))
        i = i + 1
        dc_cp.append(send(d_send.at[y_, :, :, low], d_recv.at[y_, :, :, low], dc_ss.at[i], dc_rs.at[i], other))

    transform(2, r_late)

    for copy in dt_cp:
        copy.wait_recv()
    xs = ((1 - xhi, xlo), (xhi, 1 - xlo), (1 - xhi, 1 - xlo))
    x1_cp, y1_cp = [], []
    for k, (h, x_) in enumerate(xs):

        def add(r, _):
            v = d_own[r, h, x_, top] + d_recv[r, h, x_, top].astype(F32)
            x1_send[k, r] = v.astype(BF)
            return 0

        lax.fori_loop(0, 4, add, 0)
        x1_cp.append(send(x1_send.at[k], x1_recv.at[k], x1_ss.at[k], x1_rs.at[k], xdev[k]))
    for q, d in enumerate(Y_ORDER):
        dc_cp[q].wait_recv()
        if d:

            def add(r, _):
                h, x_ = r // 2, r % 2
                v = d_own[(y + d) % 4, h, x_, low] + d_recv[(y + d) % 4, h, x_, low].astype(F32)
                y1_send[q, h, x_] = v.astype(BF)
                return 0

            lax.fori_loop(0, 4, add, 0)
            y1_cp.append(send(y1_send.at[q], y1_recv.at[q], y1_ss.at[q], y1_rs.at[q], ydev[d]))

    pl.semaphore_wait(word.at[3], 1)
    o_cp = []

    def blocks(q):
        d = Y_ORDER[q]
        y_, lo, hi = columns(d)
        left = jnp.concatenate([st[lo, :], st[hi, :]], axis=0)
        v = lax.dot_general(left, tr[...], NT, preferred_element_type=F32).astype(BF)
        o_send[q, 0] = v[:128]
        o_send[q, 1] = v[128:]
        i = 2 * q
        o_cp.append(
            send(o_send.at[q, 1 - xhi], gao_ref.at[n], o_ss.at[i], o_rs.at[i], at(z, xlo, core, 1 - xhi, y_))
        )
        if d:
            i = i + 1
            o_cp.append(send(o_send.at[q, xhi], gao_ref.at[n], o_ss.at[i], o_rs.at[i], at(z, xlo, core, xhi, y_)))

    blocks(0)
    blocks(1)
    for copy in x1_cp:
        copy.wait_recv()

    def sum_x(r, _):
        v = d_own[r, xhi, xlo, top] + d_recv[r, xhi, xlo, top].astype(F32)
        for k in range(3):
            v = v + x1_recv[k, r].astype(F32)
        e1[r] = v
        return 0

    lax.fori_loop(0, 4, sum_x, 0)
    y2_cp = []
    for d in (1, 2, 3):
        y2_send[d - 1] = e1[(y + d) % 4].astype(BF)
        y2_cp.append(send(y2_send.at[d - 1], y2_recv.at[d - 1], y2_ss.at[d - 1], y2_rs.at[d - 1], ydev[d]))
    for copy in y1_cp:
        copy.wait_recv()

    def sum_y(r, _):
        h, x_ = r // 2, r % 2
        v = d_own[y, h, x_, low] + d_recv[y, h, x_, low].astype(F32)
        for k in range(3):
            v = v + y1_recv[k, h, x_].astype(F32)
        e0[h, x_] = v
        return 0

    lax.fori_loop(0, 4, sum_y, 0)
    x2_cp = []
    for k, (h, x_) in enumerate(xs):
        x2_send[k] = e0[h, x_].astype(BF)
        x2_cp.append(send(x2_send.at[k], x2_recv.at[k], x2_ss.at[k], x2_rs.at[k], xdev[k]))
    blocks(2)
    for copy in y2_cp + x2_cp:
        copy.wait_recv()
    v0, v1 = e0[xhi, xlo], e1[y]
    for k in range(3):
        v0 = v0 + x2_recv[k].astype(F32)
        v1 = v1 + y2_recv[k].astype(F32)
    dz[0:2] = v0.reshape(2, 4, 16, 128)
    dz[2:4] = v1.reshape(2, 4, 16, 128)
    pl.semaphore_wait(word.at[2], 2)
    dl_cp = []
    for d in (1, 2, 3):
        dl_send[d - 1] = dz[:, (l + d) % 4].astype(BF)
        dl_cp.append(send(dl_send.at[d - 1], dl_recv.at[d - 1], dl_ss.at[d - 1], dl_rs.at[d - 1], ldev[d]))
    blocks(3)
    own_copy = pltpu.make_async_copy(o_send.at[3, xhi], gao_ref.at[n], local_sem.at[2])
    own_copy.start()
    for copy in dl_cp:
        copy.wait_recv()
    v = dz[:, l]
    for k in range(3):
        v = v + dl_recv[k].astype(F32)
    dg[...] = v
    dg_cp = []
    for d in (1, 2, 3):
        dg_cp.append(send(dg.at[(g + d) % 4], dg_recv.at[d - 1], dg_ss.at[d - 1], dg_rs.at[d - 1], gdev[d]))
    for copy in dg_cp:
        copy.wait_recv()
    v = dg[g]
    for k in range(3):
        v = v + dg_recv[k]
    dens_ref[...] = v * (1.0 / PAIRS)

    own_copy.wait()
    for copy in o_cp:
        copy.wait_recv()
    for copy in started:
        copy.wait_send()

    slab_copy(s_early).wait_send()
    slab_copy(s_late).wait_send()
    for k in range(4):
        quarter(k).wait_send()


def on_device(b_blocks, occ_energy, vir_energy, coef_vir):
    dma = pltpu.SemaphoreType.DMA
    vm = pltpu.VMEM
    scratch = [
        vm((NV, NAUX), BF),
        vm((STEPS, SLAB, NAUX), BF),
        vm((8, 128), F32),
        vm((STEPS, 8, 128), F32),
        vm((8, 128, NV), BF),
        vm((NV, 128), F32),
        vm((NV, STEPS * SLAB), BF),
        vm((NAO, STEPS * SLAB), BF),
        vm((NAUX, STEPS * SLAB), BF),
        vm((4, 2, 2, 16, 16, 128), F32),
        vm((4, 2, 2, 16, 16, 128), BF),
        vm((4, 2, 2, 16, 16, 128), BF),
        vm((3, 2, 2, 8, 16, 128), BF),
        vm((3, 2, 2, 8, 16, 128), BF),
        vm((3, 4, 8, 16, 128), BF),
        vm((3, 4, 8, 16, 128), BF),
        vm((2, 2, 8, 16, 128), F32),
        vm((4, 8, 16, 128), F32),
        vm((3, 8, 16, 128), BF),
        vm((3, 8, 16, 128), BF),
        vm((3, 8, 16, 128), BF),
        vm((3, 8, 16, 128), BF),
        vm((4, 4, 16, 128), F32),
        vm((3, 4, 16, 128), BF),
        vm((3, 4, 16, 128), BF),
        vm((4, 16, 128), F32),
        vm((3, 16, 128), F32),
        vm((1, NV), F32),
        vm((4, 2, 128, NAO), BF),
        vm((4, NV, 256), F32),
        pltpu.SemaphoreType.REGULAR((4,)),
        dma((4,)),
    ]
    for count in (3, 3, 7, 7, 8, 3, 3, 3, 3, 3, 3, 8, 8):
        scratch += [dma((count,)), dma((count,))]
    return pl.pallas_call(
        kernel,
        out_shape=(
            jax.ShapeDtypeStruct((16, 128), F32),
            jax.ShapeDtypeStruct((8, 128, NAO), BF),
        ),
        in_specs=[
            pl.BlockSpec(memory_space=pltpu.HBM),
            pl.BlockSpec(memory_space=pltpu.SMEM),
            pl.BlockSpec(memory_space=pltpu.HBM),
            pl.BlockSpec(memory_space=pltpu.HBM),
        ],
        out_specs=(
            pl.BlockSpec(memory_space=pltpu.VMEM),
            pl.BlockSpec(memory_space=pl.ANY),
        ),
        scratch_shapes=scratch,
        compiler_params=pltpu.CompilerParams(
            collective_id=0, has_side_effects=True, vmem_limit_bytes=50 * 1024 * 1024
        ),
    )(b_blocks, occ_energy, vir_energy.reshape(1, NV), coef_vir)


def solution(mesh):
    return jax.shard_map(
        on_device,
        mesh=mesh,
        in_specs=(P(("wide", "narrow"), None, None), P(("wide", "narrow")), P(), P("narrow", None)),
        out_specs=(P("wide", "narrow"), P("wide", "narrow", None)),
        check_vma=False,
    )
```

time: 101 us -> 97.6 us (0.966)
  the two profiles are of different devices: /device:TPU:32 before, /device:TPU:6 now
where the time goes in v2:
time: 97.6 us; the launch traced here: 97.4 us
  Pallas kernels  92.5 us (95%)
  local copies, waits for them, and re-layouts  3.55 us (4%)
  between operations  1.29 us (1%)
    pallas_call x1, Pallas kernels, on_device(): pl.pallas_call(kernel, out_shape=(jax.ShapeDtypeStruct((16, 128), F32), j...  92.5 us
    unnamed x6, local copies, waits for them, and re-layouts  3.55 us

profile of v2, /device:TPU:6, one launch (start us, length us, event | category | flops | bytes accessed | tf_op | source)
XLA Modules:
  0.0 97.4 jit_solution(15054207099560945098)
XLA Ops:
  1.3 0.0 copy-start
  1.3 0.9 copy-done
  2.2 0.0 copy-start.1
  2.2 0.7 copy-done.1
  2.9 92.5 %shard_map.59 = (f32[16,128]{1,0:T(8,128)S(1)}, bf16[8,128,1024]{2,1,0:T(8,128)(2,1)S(1)}) custom-call(bf16[1,1024,1024]{2,1,0:T(8,128)(2,1)} %b_hbm.1, f32[1]{0:T(128)S(6)} %copy.8.occ_ref, f32[1,1024]{1,0:T(1,128)S(1)} %bitcast.1, bf16[128,1024]{1,0:T(8,128)(2,1)S(1)} %copy-done), custom_call_target="tpu_custom_call" | custom-call | tf_op jit(solution)/shard_map/pallas_call | solution.py:431
  95.4 0.6 copy.9
  96.0 1.3 %copy.10 = bf16[8,128,1024]{2,1,0:T(8,128)(2,1)} copy(bf16[8,128,1024]{2,1,0:T(8,128)(2,1)S(1)} %get-tuple-element.5) | data formatting | bytes 4194304
Async XLA Ops:
  1.3 1.0 copy-start
  2.2 0.7 copy-start.1

commit v3 on v2

--- a/solution.py
+++ b/solution.py
@@ -37,6 +37,8 @@
     d_own,
     d_send,
     d_recv,
+    zp_send,
+    zp_recv,
     y1_send,
     y1_recv,
     x1_send,
@@ -67,6 +69,8 @@
     f_rs,
     dc_ss,
     dc_rs,
+    zp_ss,
+    zp_rs,
     y1_ss,
     y1_rs,
     x1_ss,
@@ -246,53 +250,7 @@
         d_acc[q] = lax.dot_general(amp[:, : 2 * SLAB], right, NT, preferred_element_type=F32)
     couple(2, r_late)
 
-    top, low = pl.ds(8, 8), pl.ds(0, 8)
-    dt_cp, dc_cp = [], []
-    for q, d in enumerate(Y_ORDER):
-        y_, lo, hi = columns(d)
-        right = jnp.concatenate([amp[lo, 2 * SLAB :], amp[hi, 2 * SLAB :]], axis=0)
-        v = d_acc[q] + lax.dot_general(amp[:, 2 * SLAB :], right, NT, preferred_element_type=F32)
-        v = v.reshape(16, 2, 2, 16, 256)
-        v0, v1 = v[:, :, 0], v[:, :, 1]
-        keep = jnp.where(core == 0, v0, v1)
-        give = jnp.where(core == 0, v1, v0).astype(BF)
-        for h in range(2):
-            for x_ in range(2):
-                d_own[y_, h, x_] = keep[:, x_, :, h * 128 : (h + 1) * 128]
-                d_send[y_, h, x_] = give[:, x_, :, h * 128 : (h + 1) * 128]
-        i = 2 * q
-        dt_cp.append(send(d_send.at[y_, :, :, top], d_recv.at[y_, :, :, top], dc_ss.at[i], dc_rs.at[i], other))
-        i = i + 1
-        dc_cp.append(send(d_send.at[y_, :, :, low], d_recv.at[y_, :, :, low], dc_ss.at[i], dc_rs.at[i], other))
-
     transform(2, r_late)
-
-    for copy in dt_cp:
-        copy.wait_recv()
-    xs = ((1 - xhi, xlo), (xhi, 1 - xlo), (1 - xhi, 1 - xlo))
-    x1_cp, y1_cp = [], []
-    for k, (h, x_) in enumerate(xs):
-
-        def add(r, _):
-            v = d_own[r, h, x_, top] + d_recv[r, h, x_, top].astype(F32)
-            x1_send[k, r] = v.astype(BF)
-            return 0
-
-        lax.fori_loop(0, 4, add, 0)
-        x1_cp.append(send(x1_send.at[k], x1_recv.at[k], x1_ss.at[k], x1_rs.at[k], xdev[k]))
-    for q, d in enumerate(Y_ORDER):
-        dc_cp[q].wait_recv()
-        if d:
-
-            def add(r, _):
-                h, x_ = r // 2, r % 2
-                v = d_own[(y + d) % 4, h, x_, low] + d_recv[(y + d) % 4, h, x_, low].astype(F32)
-                y1_send[q, h, x_] = v.astype(BF)
-                return 0
-
-            lax.fori_loop(0, 4, add, 0)
-            y1_cp.append(send(y1_send.at[q], y1_recv.at[q], y1_ss.at[q], y1_rs.at[q], ydev[d]))
-
     pl.semaphore_wait(word.at[3], 1)
     o_cp = []
 
@@ -311,13 +269,78 @@
             i = i + 1
             o_cp.append(send(o_send.at[q, xhi], gao_ref.at[n], o_ss.at[i], o_rs.at[i], at(z, xlo, core, xhi, y_)))
 
-    blocks(0)
-    blocks(1)
+    for q in range(4):
+        blocks(q)
+    own_copy = pltpu.make_async_copy(o_send.at[3, xhi], gao_ref.at[n], local_sem.at[2])
+    own_copy.start()
+    top, low = pl.ds(4, 4), pl.ds(0, 4)
+    par = z % 2
+    dt_cp, dc_cp = [], []
+    for q, d in enumerate(Y_ORDER):
+        y_, lo, hi = columns(d)
+        right = jnp.concatenate([amp[lo, 2 * SLAB :], amp[hi, 2 * SLAB :]], axis=0)
+        v = d_acc[q] + lax.dot_general(amp[:, 2 * SLAB :], right, NT, preferred_element_type=F32)
+        v = v.reshape(8, 2, 2, 2, 16, 256)
+        v0, v1 = v[:, :, :, 0], v[:, :, :, 1]
+        keep = jnp.where(core == 0, v0, v1)
+        give = jnp.where(core == 0, v1, v0).astype(BF)
+        for h in range(2):
+            for x_ in range(2):
+                for p in range(2):
+                    d_own[y_, h, x_, p] = keep[:, p, x_, :, h * 128 : (h + 1) * 128]
+                    d_send[y_, h, x_, p] = give[:, p, x_, :, h * 128 : (h + 1) * 128]
+        for i, p, cps in ((2 * q, 1 - par, dt_cp), (2 * q + 1, par, dc_cp)):
+            cps.append(send(d_send.at[y_, :, :, p], d_recv.at[y_, :, :, p], dc_ss.at[i], dc_rs.at[i], other))
+
+
+    for copy in dt_cp:
+        copy.wait_recv()
+    step = 1 - 2 * par
+    zdev = [((w + 64 + 4 * step) % 64, n), ((w + 64 - 4 * step) % 64, n)]
+    zp_cp = []
+    for k in range(2):
+
+        def add(r, _):
+            h, x_ = r // 2, r % 2
+            for i in range(2):
+                v = d_own[2 * k + i, h, x_, 1 - par] + d_recv[2 * k + i, h, x_, 1 - par].astype(F32)
+                zp_send[k, i, h, x_] = v.astype(BF)
+            return 0
+
+        lax.fori_loop(0, 4, add, 0)
+        zp_cp.append(send(zp_send.at[k], zp_recv.at[k], zp_ss.at[k], zp_rs.at[k], zdev[k]))
+
+    for copy in dc_cp + zp_cp:
+        copy.wait_recv()
+
+    def have(y_, h, x_, part):
+        v = d_own[y_, h, x_, par, part] + d_recv[y_, h, x_, par, part].astype(F32)
+        return v + zp_recv[y_ // 2, y_ % 2, h, x_, part].astype(F32)
+
+    xs = ((1 - xhi, xlo), (xhi, 1 - xlo), (1 - xhi, 1 - xlo))
+    x1_cp, y1_cp = [], []
+    for k, (h, x_) in enumerate(xs):
+
+        def add(r, _):
+            x1_send[k, r] = have(r, h, x_, top).astype(BF)
+            return 0
+
+        lax.fori_loop(0, 4, add, 0)
+        x1_cp.append(send(x1_send.at[k], x1_recv.at[k], x1_ss.at[k], x1_rs.at[k], xdev[k]))
+    for q, d in enumerate(Y_ORDER[:3]):
+
+        def add(r, _):
+            y1_send[q, r // 2, r % 2] = have((y + d) % 4, r // 2, r % 2, low).astype(BF)
+            return 0
+
+        lax.fori_loop(0, 4, add, 0)
+        y1_cp.append(send(y1_send.at[q], y1_recv.at[q], y1_ss.at[q], y1_rs.at[q], ydev[d]))
+
     for copy in x1_cp:
         copy.wait_recv()
 
     def sum_x(r, _):
-        v = d_own[r, xhi, xlo, top] + d_recv[r, xhi, xlo, top].astype(F32)
+        v = have(r, xhi, xlo, top)
         for k in range(3):
             v = v + x1_recv[k, r].astype(F32)
         e1[r] = v
@@ -333,7 +356,7 @@
 
     def sum_y(r, _):
         h, x_ = r // 2, r % 2
-        v = d_own[y, h, x_, low] + d_recv[y, h, x_, low].astype(F32)
+        v = have(y, h, x_, low)
         for k in range(3):
             v = v + y1_recv[k, h, x_].astype(F32)
         e0[h, x_] = v
@@ -344,29 +367,20 @@
     for k, (h, x_) in enumerate(xs):
         x2_send[k] = e0[h, x_].astype(BF)
         x2_cp.append(send(x2_send.at[k], x2_recv.at[k], x2_ss.at[k], x2_rs.at[k], xdev[k]))
-    blocks(2)
     for copy in y2_cp + x2_cp:
         copy.wait_recv()
     v0, v1 = e0[xhi, xlo], e1[y]
     for k in range(3):
         v0 = v0 + x2_recv[k].astype(F32)
         v1 = v1 + y2_recv[k].astype(F32)
-    dz[0:2] = v0.reshape(2, 4, 16, 128)
-    dz[2:4] = v1.reshape(2, 4, 16, 128)
+    dz[0:2] = v0.reshape(2, 2, 16, 128)
+    dz[2:4] = v1.reshape(2, 2, 16, 128)
     pl.semaphore_wait(word.at[2], 2)
-    dl_cp = []
-    for d in (1, 2, 3):
-        dl_send[d - 1] = dz[:, (l + d) % 4].astype(BF)
-        dl_cp.append(send(dl_send.at[d - 1], dl_recv.at[d - 1], dl_ss.at[d - 1], dl_rs.at[d - 1], ldev[d]))
-    blocks(3)
-    own_copy = pltpu.make_async_copy(o_send.at[3, xhi], gao_ref.at[n], local_sem.at[2])
-    own_copy.start()
-    for copy in dl_cp:
-        copy.wait_recv()
-    v = dz[:, l]
-    for k in range(3):
-        v = v + dl_recv[k].astype(F32)
-    dg[...] = v
+    m = l // 2
+    dl_send[...] = dz[:, 1 - m].astype(BF)
+    dl_cp = send(dl_send, dl_recv, dl_ss.at[0], dl_rs.at[0], ldev[2])
+    dl_cp.wait_recv()
+    dg[...] = dz[:, m] + dl_recv[...].astype(F32)
     dg_cp = []
     for d in (1, 2, 3):
         dg_cp.append(send(dg.at[(g + d) % 4], dg_recv.at[d - 1], dg_ss.at[d - 1], dg_rs.at[d - 1], gdev[d]))
@@ -402,22 +416,24 @@
         vm((NV, STEPS * SLAB), BF),
         vm((NAO, STEPS * SLAB), BF),
         vm((NAUX, STEPS * SLAB), BF),
-        vm((4, 2, 2, 16, 16, 128), F32),
-        vm((4, 2, 2, 16, 16, 128), BF),
-        vm((4, 2, 2, 16, 16, 128), BF),
-        vm((3, 2, 2, 8, 16, 128), BF),
-        vm((3, 2, 2, 8, 16, 128), BF),
-        vm((3, 4, 8, 16, 128), BF),
-        vm((3, 4, 8, 16, 128), BF),
-        vm((2, 2, 8, 16, 128), F32),
-        vm((4, 8, 16, 128), F32),
-        vm((3, 8, 16, 128), BF),
-        vm((3, 8, 16, 128), BF),
-        vm((3, 8, 16, 128), BF),
-        vm((3, 8, 16, 128), BF),
+        vm((4, 2, 2, 2, 8, 16, 128), F32),
+        vm((4, 2, 2, 2, 8, 16, 128), BF),
+        vm((4, 2, 2, 2, 8, 16, 128), BF),
+        vm((2, 2, 2, 2, 8, 16, 128), BF),
+        vm((2, 2, 2, 2, 8, 16, 128), BF),
+        vm((3, 2, 2, 4, 16, 128), BF),
+        vm((3, 2, 2, 4, 16, 128), BF),
+        vm((3, 4, 4, 16, 128), BF),
+        vm((3, 4, 4, 16, 128), BF),
+        vm((2, 2, 4, 16, 128), F32),
         vm((4, 4, 16, 128), F32),
         vm((3, 4, 16, 128), BF),
         vm((3, 4, 16, 128), BF),
+        vm((3, 4, 16, 128), BF),
+        vm((3, 4, 16, 128), BF),
+        vm((4, 2, 16, 128), F32),
+        vm((4, 16, 128), BF),
+        vm((4, 16, 128), BF),
         vm((4, 16, 128), F32),
         vm((3, 16, 128), F32),
         vm((1, NV), F32),
@@ -426,7 +442,7 @@
         pltpu.SemaphoreType.REGULAR((4,)),
         dma((4,)),
     ]
-    for count in (3, 3, 7, 7, 8, 3, 3, 3, 3, 3, 3, 8, 8):
+    for count in (3, 3, 7, 7, 8, 2, 3, 3, 3, 3, 1, 3, 8, 8):
         scratch += [dma((count,)), dma((count,))]
     return pl.pallas_call(
         kernel,

time: 97.6 us -> 94.3 us (0.966)
  Pallas kernels: 92.5 us -> 88.4 us
    pallas_call x1, Pallas kernels: 92.5 us -> 88.4 us  [on_device(): pl.pallas_call(kernel, out_shape=(jax.ShapeDtypeStruct((16, 128), F32), j...]
where the time goes in v3:
time: 94.3 us; the launch traced here: 93.2 us
  Pallas kernels  88.4 us (94%)
  local copies, waits for them, and re-layouts  3.55 us (4%)
  between operations  1.29 us (1%)
    pallas_call x1, Pallas kernels, on_device(): pl.pallas_call(kernel, out_shape=(jax.ShapeDtypeStruct((16, 128), F32), j...  88.4 us
    unnamed x6, local copies, waits for them, and re-layouts  3.55 us

profile of v3, /device:TPU:6, one launch (start us, length us, event | category | flops | bytes accessed | tf_op | source)
XLA Modules:
  0.0 93.2 jit_solution(14251517965308350352)
XLA Ops:
  1.3 0.0 copy-start
  1.3 0.9 %copy-done = bf16[128,1024]{1,0:T(8,128)(2,1)S(1)} copy-done((bf16[128,1024]{1,0:T(8,128)(2,1)S(1)}, bf16[128,1024]{1,0:T(8,128)(2,1)}, u32[]{:S(2)}) %copy-start) | copy-done | bytes 262168
  2.2 0.0 copy-start.1
  2.2 0.7 copy-done.1
  2.9 88.4 %shard_map.59 = (f32[16,128]{1,0:T(8,128)S(1)}, bf16[8,128,1024]{2,1,0:T(8,128)(2,1)S(1)}) custom-call(bf16[1,1024,1024]{2,1,0:T(8,128)(2,1)} %b_hbm.1, f32[1]{0:T(128)S(6)} %copy.8.occ_ref, f32[1,1024]{1,0:T(1,128)S(1)} %bitcast.1, bf16[128,1024]{1,0:T(8,128)(2,1)S(1)} %copy-done), custom_call_target="tpu_custom_call" | custom-call | tf_op jit(solution)/shard_map/pallas_call | solution.py:447
  91.3 0.6 copy.9
  91.9 1.3 %copy.10 = bf16[8,128,1024]{2,1,0:T(8,128)(2,1)} copy(bf16[8,128,1024]{2,1,0:T(8,128)(2,1)S(1)} %get-tuple-element.5) | data formatting | bytes 4194304
Async XLA Ops:
  1.3 1.0 %copy-start = (bf16[128,1024]{1,0:T(8,128)(2,1)S(1)}, bf16[128,1024]{1,0:T(8,128)(2,1)}, u32[]{:S(2)}) copy-start(bf16[128,1024]{1,0:T(8,128)(2,1)} %coef_hbm.1) | copy-start | bytes 786436
  2.2 0.7 copy-start.1

commit v4 on v3

--- a/solution.py
+++ b/solution.py
@@ -169,10 +169,9 @@
             device_id_type=MESH,
         )
 
+    slab_copy(s_early).start()
     for k in range(4):
         quarter(k).start()
-
-    slab_copy(s_early).start()
     slab_copy(s_late).start()
     pass_word(0, along(1))
     pass_word(3, [xdev[0]])

time: 94.3 us -> 91.9 us (0.975)
  Pallas kernels: 88.4 us -> 85.8 us
    pallas_call x1, Pallas kernels: 88.4 us -> 85.8 us  [on_device(): pl.pallas_call(kernel, out_shape=(jax.ShapeDtypeStruct((16, 128), F32), j...]
where the time goes in v4:
time: 91.9 us; the launch traced here: 90.6 us
  Pallas kernels  85.8 us (93%)
  local copies, waits for them, and re-layouts  3.55 us (4%)
  between operations  1.29 us (1%)
    pallas_call x1, Pallas kernels, on_device(): pl.pallas_call(kernel, out_shape=(jax.ShapeDtypeStruct((16, 128), F32), j...  85.8 us
    unnamed x6, local copies, waits for them, and re-layouts  3.55 us

profile of v4, /device:TPU:6, one launch (start us, length us, event | category | flops | bytes accessed | tf_op | source)
XLA Modules:
  0.0 90.6 jit_solution(8322891426413491549)
XLA Ops:
  1.3 0.0 copy-start
  1.3 0.9 %copy-done = bf16[128,1024]{1,0:T(8,128)(2,1)S(1)} copy-done((bf16[128,1024]{1,0:T(8,128)(2,1)S(1)}, bf16[128,1024]{1,0:T(8,128)(2,1)}, u32[]{:S(2)}) %copy-start) | copy-done | bytes 262168
  2.2 0.0 copy-start.1
  2.2 0.7 copy-done.1
  2.9 85.8 %shard_map.59 = (f32[16,128]{1,0:T(8,128)S(1)}, bf16[8,128,1024]{2,1,0:T(8,128)(2,1)S(1)}) custom-call(bf16[1,1024,1024]{2,1,0:T(8,128)(2,1)} %b_hbm.1, f32[1]{0:T(128)S(6)} %copy.8.occ_ref, f32[1,1024]{1,0:T(1,128)S(1)} %bitcast.1, bf16[128,1024]{1,0:T(8,128)(2,1)S(1)} %copy-done), custom_call_target="tpu_custom_call" | custom-call | tf_op jit(solution)/shard_map/pallas_call | solution.py:446
  88.7 0.6 copy.9
  89.3 1.3 %copy.10 = bf16[8,128,1024]{2,1,0:T(8,128)(2,1)} copy(bf16[8,128,1024]{2,1,0:T(8,128)(2,1)S(1)} %get-tuple-element.5) | data formatting | bytes 4194304
Async XLA Ops:
  1.3 1.0 %copy-start = (bf16[128,1024]{1,0:T(8,128)(2,1)S(1)}, bf16[128,1024]{1,0:T(8,128)(2,1)}, u32[]{:S(2)}) copy-start(bf16[128,1024]{1,0:T(8,128)(2,1)} %coef_hbm.1) | copy-start | bytes 786436
  2.2 0.7 copy-start.1
